TPU v7x, 128 devices: a whole 4x4x4 slice. The times are simulated.
128 devices in a mesh: tm: 32 (over y, x, core), stream: 4 (over z).
Axes of the slice: x: 4, y: 4, z: 4, core: 2. Of those that a mesh axis runs over, the one named last changes fastest.
Arguments:
- raw: bfloat16 [4, 6, 524288], P('stream', None, 'tm'), may hold values from -6 to 6
- starts: int32 [4, 131072], P('stream', 'tm'), may hold values from 0 to 1, as said below
- neg_owner: int32 [4, 1024, 4], P('stream', 'tm'), may hold values from 0 to 127, all different within a row; in each aligned block of 32 rows (0 to 31, 32 to 63, ..., all dimensions but the last counted through in order) at most 2 rows name the same one
- neg_block: int32 [4, 1024, 4], P('stream', 'tm'), may hold values from 0 to 31
- enc_weight: bfloat16 [24, 256], replicated, may hold values from -1.25 to 1.25
- tcn_weight: bfloat16 [4, 2, 256, 256], replicated, may hold values from -0.25 to 0.25
- pred_weight: bfloat16 [256, 256], replicated, may hold values from -0.375 to 0.375
Outputs:
- grad_latent: float32 [4, 131072, 256], P('stream', 'tm')
Inputs may be any that keep to these rules, and one draw needn't show every extreme that they name: `starts`: row 0 of every stream is 1. `neg_owner`: the owner is the flat device index tm * 4 + stream; each row names 4 different owners; within the 32 rows of one device no owner is named more than 2 times, a bound that some block reaches.
All inputs are finite; a program needn't handle non-finite values.
Results may differ from a plain program's by a relative error of at most 0.011.
Values may be sent and summed in bfloat16 or wider, within the bound.
No kernel may reach another device: no remote copies, remote signals or barrier semaphores. Data moves between devices by JAX's collectives and lax.ppermute only.
A program may use at most 192 MiB of HBM per device.

v0:
```python
import jax
import jax.numpy as jnp
from jax import lax
from jax.experimental import pallas as pl
from jax.experimental.pallas import tpu as pltpu
from jax.sharding import PartitionSpec as P

BLOCK = 128
NEG = 4
HALO = 32
AHEAD = 4
CAP = 2
LAYERS = 4
PACK = 32
TOGETHER = 16
PAIRED = 1
PIECES = 4
SKEW = 1
GATHERED = 64
CHUNK = 1024
NOTE = 95
LEAD = 20
SEGMENT = 512
SCORED = 4
SCALE = 10.0
EPSILON = 1e-06
BF = jnp.bfloat16
F32 = jnp.float32
MIB = 1 << 20
VMEM = 60 * MIB


def dot(a, b):
    return jnp.dot(a, b, preferred_element_type=F32)


def dot_nt(a, b):
    return lax.dot_general(a, b, (((1,), (1,)), ((), ())), preferred_element_type=F32)


def row_sum(x):
    return jnp.sum(x, axis=-1, keepdims=True)


def silu_of_half(half):
    return half + half * jnp.tanh(half)


def wide(x):
    return jnp.concatenate([x, x], axis=1)


def prep_kernel(owner_ref, block_ref, raw_ref, starts_ref, rim_ref, enc_ref,
                pack_ref, push_ref, slot_ref, bd_ref, lines, packs, turned, seen):
    blocks = pack_ref.shape[0]
    lines[...] = jnp.zeros_like(lines)
    for b in range(blocks):
        lines[b, 0:6, :] = raw_ref[:, b * 512:(b + 1) * 512].astype(F32)
    row = lax.broadcasted_iota(jnp.int32, (512, 512), 0)
    col = lax.broadcasted_iota(jnp.int32, (512, 512), 1)
    perm = jnp.where(row == 4 * (col & 127) + (col >> 7), 1.0, 0.0).astype(BF)
    row = lax.broadcasted_iota(jnp.int32, (128, 128), 0)
    col = lax.broadcasted_iota(jnp.int32, (128, 128), 1)
    perm_halo = jnp.where(row == 4 * (col & 31) + (col >> 5), 1.0, 0.0).astype(BF)
    flat = lines[...].reshape(blocks * 8, 512).astype(BF)
    main = dot(flat, perm).reshape(blocks, 8, 512)
    halo = dot(flat[:, 384:512], perm_halo).reshape(blocks, 8, 128)
    rim = rim_ref[...]
    rim_halo = dot(rim, perm_halo)

    lane = lax.broadcasted_iota(jnp.int32, (blocks + 8, 128), 1)
    level_row = lax.broadcasted_iota(jnp.int32, (8, 128), 0)
    rim_f = rim.astype(F32)
    before = jnp.where(level_row == 7, pltpu.roll(rim_f, 1, 0), 0.0)
    started = jnp.concatenate([before, starts_ref[...].astype(F32)], axis=0)
    level = 1.0 - started
    for distance in (1, 2, 4):
        moved = pltpu.roll(started, distance, 1)
        started = jnp.maximum(
            started, jnp.where(lane < distance, pltpu.roll(moved, 1, 0), moved)
        )
        level = level + (1.0 - started)
    level_halo = jnp.where(lane < HALO, pltpu.roll(level, HALO, 1), 0.0)

    for k in range(4):
        packs[:, k * 6:(k + 1) * 6, :] = main[:, 0:6, k * 128:(k + 1) * 128]
    packs[0, 24:30, :] = rim_halo[0:6]
    packs[1:blocks, 24:30, :] = halo[0:blocks - 1, 0:6, :]
    for b in range(blocks):
        packs[b, 30:31, :] = level[8 + b:9 + b]
        packs[b, 31:32, :] = level_halo[7 + b:8 + b]
    quarter = lax.broadcasted_iota(jnp.int32, (PACK, 128), 1) >> 5
    for group in range(blocks // 4):
        four = [packs[group * 4 + q] for q in range(4)]
        parts = []
        for g in range(4):
            part = four[g]
            for q in range(4):
                if q != g:
                    part = jnp.where(quarter == q, pltpu.roll(four[q], (q - g) * 32 % 128, 1), part)
            parts.append(part)
        flipped = jnp.transpose(jnp.concatenate(parts, axis=0))
        for q in range(4):
            turned[group * 4 + q] = flipped[q * 32:(q + 1) * 32]
    pack_ref[...] = turned[...].astype(BF)

    lane = lax.broadcasted_iota(jnp.int32, (PACK, 128), 1)
    note = jnp.where(lane == NOTE, 1.0, 0.0)
    unused = (-note).astype(BF)

    def clear(i, carry):
        push_ref[i] = unused
        return carry

    lax.fori_loop(0, push_ref.shape[0], clear, 0, unroll=8)

    def forget(i, carry):
        seen[i] = 0
        return carry

    lax.fori_loop(0, seen.shape[0], forget, 0, unroll=8)

    def send(i, carry):
        owner = owner_ref[i % NEG, i // NEG]
        rank = seen[owner]
        seen[owner] = rank + 1
        slot = owner * CAP + rank
        slot_ref[i] = slot
        wanted = block_ref[i % NEG, i // NEG].astype(F32)
        push_ref[slot] = (turned[i // NEG] + note * wanted).astype(BF)
        return carry

    lax.fori_loop(0, blocks * NEG, send, 0, unroll=4)

    bd_ref[...] = jnp.zeros_like(bd_ref)
    half_enc = (enc_ref[...].astype(F32) * 0.5).astype(BF)
    for q in range(4):
        bd_ref[q * 32:q * 32 + 24, q * 256:(q + 1) * 256] = half_enc


def prep(owners, wanted, raw, starts, rim, enc_weight, owners_count):
    blocks = starts.shape[0]
    smem = pl.BlockSpec(memory_space=pltpu.SMEM)
    vmem = pl.BlockSpec(memory_space=pltpu.VMEM)
    return pl.pallas_call(
        prep_kernel,
        out_shape=(
            jax.ShapeDtypeStruct((blocks, PACK, 128), BF),
            jax.ShapeDtypeStruct((owners_count * CAP, PACK, 128), BF),
            jax.ShapeDtypeStruct((blocks * NEG,), jnp.int32),
            jax.ShapeDtypeStruct((128, 1024), BF),
        ),
        in_specs=[smem, smem, vmem, vmem, vmem, vmem],
        out_specs=(vmem, vmem, smem, vmem),
        scratch_shapes=[
            pltpu.VMEM((blocks, 8, 512), F32),
            pltpu.VMEM((blocks, PACK, 128), F32),
            pltpu.VMEM((blocks, PACK, 128), F32),
            pltpu.SMEM((owners_count,), jnp.int32),
        ],
        compiler_params=pltpu.CompilerParams(vmem_limit_bytes=VMEM),
        name="prep",
    )(owners, wanted, raw, starts, rim, enc_weight)


def halo_rows(pack):
    lane = lax.broadcasted_iota(jnp.int32, (HALO, 128), 1)
    halo = jnp.where(lane == 30, pltpu.roll(pack, 127, 1), 0.0)
    for g in range(4):
        moved = pltpu.roll(pack, (-26 * g - 24) % 128, 1)
        halo = jnp.where((lane >= 6 * g) & (lane < 6 * g + 6), moved, halo)
    return halo


def layer_half(h, level, layer, w_ref):
    moved = pltpu.roll(h, 2**layer, 0)
    gated = jnp.where(level > layer, moved, 0.0)
    return dot(h.astype(BF), w_ref[layer, 0]) + dot(gated.astype(BF), w_ref[layer, 1])


def forward_kernel(pack_ref, bd_ref, w_ref, pred_ref, lat_ref, ctx_ref, slope_ref, level_ref,
                   rim_slope_ref, rim_level_ref, keyed_ref):
    first = pl.program_id(0) == 0
    packs = pack_ref[...].reshape(4 * PACK, 128).astype(F32)
    halo = halo_rows(packs[0:PACK])
    rows = jnp.concatenate([packs, halo], axis=0)
    encoded = silu_of_half(dot(rows.astype(BF), bd_ref[...]))
    pieces, columns = [encoded[4 * PACK:, 0:256]], [halo[:, 30:31]]
    for q in range(4):
        for g in range(4):
            pieces.append(encoded[q * PACK:(q + 1) * PACK, g * 256:(g + 1) * 256])
            columns.append(packs[q * PACK:(q + 1) * PACK, g * 32 + 30:g * 32 + 31])
    latent = jnp.concatenate(pieces, axis=0).astype(BF)
    level = jnp.broadcast_to(jnp.concatenate(columns, axis=0), (HALO + SEGMENT, 256))
    level_ref[...] = level[HALO:, 0:128]
    lat_ref[...] = latent[HALO:]
    h = latent.astype(F32)
    own = h[HALO:]
    key_scale = lax.rsqrt(row_sum(own * own) + EPSILON)
    keyed_ref[...] = dot_nt((own * key_scale).astype(BF), pred_ref[...]).astype(BF)
    slopes = []
    for layer in range(LAYERS):
        half = layer_half(h, level, layer, w_ref)
        tanh = jnp.tanh(half)
        slope = (0.5 * (1.0 + tanh)) * (1.0 + half * (1.0 - tanh))
        slope_ref[layer] = slope[HALO:].astype(BF)
        slopes.append(slope[:HALO].astype(BF))
        h = h + half + half * tanh
    ctx_ref[...] = h[HALO - AHEAD:HALO - AHEAD + SEGMENT].astype(BF)

    @pl.when(first)
    def _():
        rim_level_ref[...] = level[:HALO, 0:128]
        for layer in range(LAYERS):
            rim_slope_ref[layer] = slopes[layer]


def forward(pack, bd, half_weight, pred_weight):
    rows = pack.shape[0] * BLOCK
    steps = rows // SEGMENT
    whole = lambda *shape: pl.BlockSpec(shape, lambda i: (0,) * len(shape))
    rows_of = lambda width: pl.BlockSpec((SEGMENT, width), lambda i: (i, 0))
    return pl.pallas_call(
        forward_kernel,
        grid=(steps,),
        out_shape=(
            jax.ShapeDtypeStruct((rows, 256), BF),
            jax.ShapeDtypeStruct((rows, 256), BF),
            jax.ShapeDtypeStruct((LAYERS, rows, 256), BF),
            jax.ShapeDtypeStruct((rows, 128), F32),
            jax.ShapeDtypeStruct((LAYERS, HALO, 256), BF),
            jax.ShapeDtypeStruct((HALO, 128), F32),
            jax.ShapeDtypeStruct((rows, 256), BF),
        ),
        in_specs=[
            pl.BlockSpec((4, PACK, 128), lambda i: (i, 0, 0)),
            whole(128, 1024),
            whole(LAYERS, 2, 256, 256),
            whole(256, 256),
        ],
        out_specs=(
            rows_of(256),
            rows_of(256),
            pl.BlockSpec((LAYERS, SEGMENT, 256), lambda i: (0, i, 0)),
            rows_of(128),
            whole(LAYERS, HALO, 256),
            whole(HALO, 128),
            rows_of(256),
        ),
        compiler_params=pltpu.CompilerParams(vmem_limit_bytes=VMEM),
        cost_estimate=pl.CostEstimate(
            flops=rows * 2 * 65536 * 10, bytes_accessed=18 * MIB, transcendentals=rows * 256 * 5
        ),
        name="forward",
    )(pack, bd, half_weight, pred_weight)


def kept(count, half):
    shared = ((count - half + 63) >> 6) << 5
    return jnp.where(count > half, jnp.minimum(count, half + shared), count)


def answer_kernel(push_ref, pack_ref, answer_ref, order_ref, bounds_ref, wanted_ref, extra_ref,
                  listed, arrived):
    slots = push_ref.shape[0]
    half = slots // 2
    notes = push_ref[:, 0:16, :].astype(F32)[:, 0, :]
    listed[...] = jnp.transpose(notes)[NOTE:NOTE + 1].astype(jnp.int32)
    pltpu.sync_copy(listed, arrived)

    def clear(i, carry):
        order_ref[i] = 0
        return carry

    lax.fori_loop(0, slots, clear, 0, unroll=8)

    def reply(i, count):
        wanted = arrived[0, i]
        wanted_ref[i] = jnp.maximum(wanted, 0)
        answer_ref[i] = pack_ref[jnp.maximum(wanted, 0)]
        order_ref[count] = i
        return count + jnp.where(wanted >= 0, 1, 0)

    count = lax.fori_loop(0, slots, reply, 0, unroll=8)
    bounds_ref[0] = 0
    bounds_ref[1] = kept(count, half)
    bounds_ref[2] = count
    extra_ref[...] = jnp.zeros_like(extra_ref)
    extra_ref[half] = jnp.full((PACK, 128), count.astype(F32)).astype(BF)

    def share(i, carry):
        extra_ref[i - half] = push_ref[order_ref[i]]
        return carry

    lax.fori_loop(half, jnp.maximum(count, half), share, 0)


def answer(pushed, pack):
    slots = pushed.shape[0]
    smem = pl.BlockSpec(memory_space=pltpu.SMEM)
    vmem = pl.BlockSpec(memory_space=pltpu.VMEM)
    return pl.pallas_call(
        answer_kernel,
        out_shape=(
            jax.ShapeDtypeStruct((slots, PACK, 128), BF),
            jax.ShapeDtypeStruct((slots + 8,), jnp.int32),
            jax.ShapeDtypeStruct((3,), jnp.int32),
            jax.ShapeDtypeStruct((slots,), jnp.int32),
            jax.ShapeDtypeStruct((slots // 2 + 1, PACK, 128), BF),
        ),
        in_specs=[vmem, vmem],
        out_specs=(vmem, smem, smem, smem, vmem),
        scratch_shapes=[pltpu.VMEM((1, slots), jnp.int32), pltpu.SMEM((1, slots), jnp.int32)],
        compiler_params=pltpu.CompilerParams(vmem_limit_bytes=VMEM),
        name="answer",
    )(pushed, pack)


def request_stages(base, order_ref, push_ref, bd_ref, w_ref, ctx_ref, first_out,
                   patches, level, here, there, left, right, gated, half_ref):
    times = LEAD + BLOCK - AHEAD

    def pieces(first, parts=PIECES):
        edges = [first + (times - first) * p // parts for p in range(parts + 1)]
        return [(a * TOGETHER, b * TOGETHER) for a, b in zip(edges[:-1], edges[1:])]

    def parts(a, b):
        return [slice(c, min(c + 32, b)) for c in range(a, b, 32)]

    for j in range(TOGETHER):
        pack = push_ref[order_ref[base + j]].astype(F32)
        patches[pl.ds(j, LEAD, stride=TOGETHER), :] = halo_rows(pack)[HALO - LEAD:]
        for g in range(4):
            count = min(32, BLOCK - AHEAD - g * 32)
            own = pltpu.roll(pack, -32 * g % 128, 1) if g else pack
            at = (LEAD + g * 32) * TOGETHER + j
            patches[pl.ds(at, count, stride=TOGETHER), :] = own[:count]
        if j % 4 == 3:
            yield
    enc = bd_ref[:, 0:256]
    for a, b in pieces(0):
        half_ref[a:b, :] = dot(patches[a:b, :].astype(BF), enc).astype(BF)
        yield
        level[a:b, :] = jnp.broadcast_to(patches[a:b, 30:31], (b - a, 128)).astype(BF)
        for at in parts(a, b):
            here[at, :] = silu_of_half(half_ref[at, :])
        yield
    source, target = here, there
    first = 0
    for layer in range(LAYERS):
        first += 2**layer if layer else 2
        back = 2**layer * TOGETHER
        both = w_ref[layer].reshape(512, 256)
        for a, b in pieces(first):
            for at in parts(a, b):
                gate = jnp.minimum(jnp.maximum(level[at, :] - float(layer), 0.0), 1.0)
                gated[at, :] = source[at.start - back:at.stop - back, :] * wide(gate)
            yield
            x = jnp.concatenate([source[a:b, :], gated[a:b, :]], axis=1)
            half_ref[a:b, :] = dot(x, both).astype(BF)
            yield
            for at in parts(a, b):
                result = source[at, :] + silu_of_half(half_ref[at, :])
                if layer < LAYERS - 1:
                    target[at, :] = result
                else:
                    result = result.astype(F32)
                    to = slice(at.start - first * TOGETHER, at.stop - first * TOGETHER)
                    left[to, :] = result[:, 0:128]
                    right[to, :] = result[:, 128:256]
            yield
        source, target = target, source
    for j in range(TOGETHER):
        rows = pl.ds(j, BLOCK, stride=TOGETHER)
        ctx_ref[first_out + j] = jnp.concatenate([left[rows, :], right[rows, :]], axis=1).astype(BF)
        if j % 4 == 3:
            yield


def recompute_kernel(order_ref, bounds_ref, push_ref, bd_ref, w_ref, ctx_ref, *scratch):
    base = bounds_ref[0] + pl.program_id(0) * PAIRED * TOGETHER

    @pl.when(base < bounds_ref[1])
    def _():
        each = len(scratch) // PAIRED
        waiting = [
            request_stages(
                base + p * TOGETHER, order_ref, push_ref, bd_ref, w_ref, ctx_ref, p * TOGETHER,
                *scratch[p * each:(p + 1) * each],
            )
            for p in range(PAIRED)
        ]
        for p, stages in enumerate(waiting):
            for _ in range(SKEW * (PAIRED - 1 - p)):
                next(stages)
        while waiting:
            waiting = [stages for stages in waiting if next(stages, True) is None]


def last_step(count, together):
    return jnp.maximum(count - 1, 0) // together


def recompute(order, bounds, pushed, bd, half_weight):
    slots = order.shape[0] // TOGETHER * TOGETHER
    together = PAIRED * TOGETHER
    times = LEAD + BLOCK - AHEAD
    whole = lambda *shape: pl.BlockSpec(shape, lambda i, o, c: (0,) * len(shape))
    return pl.pallas_call(
        recompute_kernel,
        grid_spec=pltpu.PrefetchScalarGridSpec(
            num_scalar_prefetch=2,
            grid=(slots // TOGETHER // PAIRED,),
            in_specs=[whole(*pushed.shape), whole(128, 1024), whole(LAYERS, 2, 256, 256)],
            out_specs=pl.BlockSpec(
                (together, BLOCK, 256),
                lambda i, o, c: (
                    jnp.minimum(c[0] // together + i, last_step(c[1], together)), 0, 0
                ),
            ),
            scratch_shapes=[
                pltpu.VMEM((times * TOGETHER, 128), F32),
                pltpu.VMEM((times * TOGETHER, 128), BF),
                pltpu.VMEM((times * TOGETHER, 256), BF),
                pltpu.VMEM((times * TOGETHER, 256), BF),
                pltpu.VMEM((BLOCK * TOGETHER, 128), F32),
                pltpu.VMEM((BLOCK * TOGETHER, 128), F32),
                pltpu.VMEM((times * TOGETHER, 256), BF),
                pltpu.VMEM((times * TOGETHER, 256), BF),
            ] * PAIRED,
        ),
        out_shape=jax.ShapeDtypeStruct((slots, BLOCK, 256), BF),
        compiler_params=pltpu.CompilerParams(vmem_limit_bytes=VMEM),
        cost_estimate=pl.CostEstimate(
            flops=slots * 160 * 2 * 65536 * 10, bytes_accessed=20 * MIB,
            transcendentals=slots * 160 * 256 * 5,
        ),
        name="recompute",
    )(order, bounds, pushed, bd, half_weight)


def score_kernel(slot_ref, answer_ref, ctx_ref, lat_ref, level_ref, pred_ref, bd_ref,
                 pred_grad_ref, target_grad_ref, stats_ref):
    step = pl.program_id(0)

    @pl.when(step == 0)
    def _():
        stats_ref[...] = jnp.zeros_like(stats_ref)

    blocks = range(SCORED)
    slots = [slot_ref[step * SCORED * NEG + i] for i in range(SCORED * NEG)]
    lane = lax.broadcasted_iota(jnp.int32, (BLOCK, 128), 1)
    ats = [slice(g * BLOCK, (g + 1) * BLOCK) for g in blocks]
    packs = [
        jnp.concatenate([answer_ref[slots[g * NEG + j]] for j in range(NEG)], axis=0) for g in blocks
    ]
    raw_pred = [dot(ctx_ref[at, :], pred_ref[...]) for at in ats]
    half = [dot(pack, bd_ref[...]) for pack in packs]
    pred_scale = [lax.rsqrt(row_sum(x * x) + EPSILON) for x in raw_pred]
    unit = [x * y for x, y in zip(raw_pred, pred_scale)]
    query = [x.astype(BF) for x in unit]
    keys = []
    for g in blocks:
        pieces = []
        for j in range(4):
            negative = silu_of_half(half[g][:, j * 256:(j + 1) * 256])
            key_scale = lax.rsqrt(row_sum(negative * negative) + EPSILON)
            pieces.append((negative * (key_scale)).astype(BF))
        keys.append(jnp.concatenate(pieces, axis=0))
    scores = [dot_nt(query[g], keys[g]) for g in blocks]
    exp_neg = [jnp.exp(SCALE * x) for x in scores]
    both = [dot(exp_neg[g].astype(BF), keys[g]) for g in blocks]
    sums = [row_sum(x) for x in exp_neg]
    columns = jnp.zeros((BLOCK, 128), F32)
    for g in blocks:
        at = ats[g]
        query_f = query[g].astype(F32)
        latent = lat_ref[at, :].astype(F32)
        usable = jnp.where(level_ref[at, 0:1] > 2.0, 1.0, 0.0)
        own_scale = lax.rsqrt(row_sum(latent * latent) + EPSILON)
        positive = SCALE * row_sum(query_f * latent) * own_scale
        exp_pos = jnp.exp(positive)
        share = usable / (exp_pos + sums[g])
        d_pos = share * exp_pos - usable
        pull = SCALE * d_pos * own_scale
        query_grad = (SCALE * share) * both[g] + (pull) * latent
        target_grad_ref[at, :] = (
            (pull) * query_f - (d_pos * positive * own_scale * own_scale) * latent
        )
        along = row_sum(unit[g] * query_grad)
        pred_grad_ref[at, :] = (
            (pred_scale[g]) * (query_grad - (along) * unit[g])
        ).astype(BF)
        columns = jnp.where(lane == 2 * g, pred_scale[g], columns)
        columns = jnp.where(lane == 2 * g + 1, share, columns)
    rows = jnp.transpose(columns)
    for i in range(SCORED * NEG):
        g = i // NEG
        stats_ref[slots[i]] = rows[2 * g:2 * g + 2]


def score(slots, answers, ctx, latents, levels, pred_weight, bd):
    rows = ctx.shape[0]
    count = answers.shape[0]
    whole = lambda *shape: pl.BlockSpec(shape, lambda i, s: (0,) * len(shape))
    rows_of = lambda width: pl.BlockSpec((SCORED * BLOCK, width), lambda i, s: (i, 0))
    return pl.pallas_call(
        score_kernel,
        grid_spec=pltpu.PrefetchScalarGridSpec(
            num_scalar_prefetch=1,
            grid=(rows // BLOCK // SCORED,),
            in_specs=[
                whole(count, PACK, 128), rows_of(256), rows_of(256), rows_of(128),
                whole(256, 256), whole(128, 1024),
            ],
            out_specs=(rows_of(256), rows_of(256), whole(count, 2, 128)),
        ),
        out_shape=(
            jax.ShapeDtypeStruct((rows, 256), BF),
            jax.ShapeDtypeStruct((rows, 256), F32),
            jax.ShapeDtypeStruct((count, 2, 128), F32),
        ),
        compiler_params=pltpu.CompilerParams(vmem_limit_bytes=VMEM),
        cost_estimate=pl.CostEstimate(
            flops=rows * 2 * 65536 * 10, bytes_accessed=16 * MIB, transcendentals=rows * 256 * 6
        ),
        name="score",
    )(slots, answers, ctx, latents, levels, pred_weight, bd)


def backward_kernel(pred_grad_ref, slope_ref, level_ref, target_grad_ref, rim_slope_ref,
                    rim_level_ref, pred_ref, w_ref, out_ref, rim_ref, carry):
    @pl.when(pl.program_id(0) == 0)
    def _():
        carry[...] = jnp.zeros_like(carry)

    def earlier(values, distance, place):
        longer = jnp.concatenate([values, carry[place]], axis=0)
        carry[place] = values[0:8]
        return longer[distance:distance + values.shape[0]]

    def through_layers(cotangent, slopes, level):
        for layer in reversed(range(LAYERS)):
            back = cotangent * slopes[layer].astype(F32)
            gated = jnp.where(level > layer, back, 0.0)
            cotangent = (
                cotangent
                + dot(
                    jnp.concatenate([back, earlier(gated, 2**layer, layer)], axis=1).astype(BF),
                    w_ref[layer].reshape(512, 256),
                )
            )
        return cotangent

    context_rows = dot(pred_grad_ref[...], pred_ref[...])
    cotangent = earlier(context_rows, AHEAD, LAYERS)
    level = wide(level_ref[...])
    out_ref[...] = through_layers(cotangent, slope_ref, level) + target_grad_ref[...]

    @pl.when(pl.program_id(0) == pl.num_programs(0) - 1)
    def _():
        cotangent = earlier(jnp.zeros((HALO, 256), F32), AHEAD, LAYERS)
        level = wide(rim_level_ref[...])
        rim_ref[...] = through_layers(cotangent, rim_slope_ref, level)


def backward(pred_grad, slopes, levels, target_grad, rim_slopes, rim_levels, pred_weight, weight):
    rows = pred_grad.shape[0]
    steps = rows // SEGMENT
    whole = lambda *shape: pl.BlockSpec(shape, lambda i: (0,) * len(shape))
    rows_of = lambda width: pl.BlockSpec((SEGMENT, width), lambda i: (steps - 1 - i, 0))
    return pl.pallas_call(
        backward_kernel,
        grid=(steps,),
        out_shape=(
            jax.ShapeDtypeStruct((rows, 256), F32),
            jax.ShapeDtypeStruct((HALO, 256), F32),
        ),
        in_specs=[
            rows_of(256),
            pl.BlockSpec((LAYERS, SEGMENT, 256), lambda i: (0, steps - 1 - i, 0)),
            rows_of(128),
            rows_of(256),
            whole(LAYERS, HALO, 256),
            whole(HALO, 128),
            whole(256, 256),
            whole(LAYERS, 2, 256, 256),
        ],
        out_specs=(rows_of(256), whole(HALO, 256)),
        scratch_shapes=[pltpu.VMEM((LAYERS + 1, 8, 256), F32)],
        compiler_params=pltpu.CompilerParams(vmem_limit_bytes=VMEM),
        cost_estimate=pl.CostEstimate(
            flops=rows * 2 * 65536 * 9, bytes_accessed=22 * MIB, transcendentals=0
        ),
        name="backward",
    )(pred_grad, slopes, levels, target_grad, rim_slopes, rim_levels, pred_weight, weight)


def own_kernel(order_ref, bounds_ref, wanted_ref, ctx_ref, help_ref, stats_ref, keyed_ref, part_ref, lat_ref,
               borrowed_ref, pred_ref, out_ref, total):
    step = pl.program_id(0)
    request_steps = pl.num_programs(0) - total.shape[0] // CHUNK

    @pl.when(step == 0)
    def _():
        total[...] = jnp.zeros_like(total)

    @pl.when((step < request_steps) & (step * GATHERED < bounds_ref[2]))
    def _():
        for part in range(0, GATHERED, 4):
            found = []
            for j in range(part, part + 4):
                at = step * GATHERED + j
                slot = order_ref[at]
                block = wanted_ref[slot]
                rows = pl.ds(pl.multiple_of(block * BLOCK, BLOCK), BLOCK)
                stats = stats_ref[slot]
                helped = jnp.where(at < bounds_ref[2], help_ref[j], jnp.zeros((BLOCK, 256), BF))
                ctx = jnp.where(at < bounds_ref[1], ctx_ref[j], helped)
                pred_scale, share = stats[0:1], stats[1:2]
                scores = dot_nt(keyed_ref[rows, :], ctx) * (SCALE * pred_scale)
                weighted = jnp.exp(scores) * (share * pred_scale)
                weighted = jnp.where(at < bounds_ref[2], weighted, 0.0)
                found.append((rows, dot(weighted.astype(BF), ctx)))
            for rows, addend in found:
                total[rows, :] += addend

    @pl.when(step >= request_steps)
    def _():
        chunk = step - request_steps
        rows = pl.ds(pl.multiple_of(chunk * CHUNK, CHUNK), CHUNK)
        direct = SCALE * dot(total[rows, :].astype(BF), pred_ref[...])
        latent = lat_ref[...].astype(F32)
        key_scale = lax.rsqrt(row_sum(latent * latent) + EPSILON)
        key = latent * key_scale
        along = row_sum(key * direct)
        out_ref[...] = part_ref[...] + key_scale * (direct - along * key)

        @pl.when(step == pl.num_programs(0) - 1)
        def _():
            out_ref[CHUNK - HALO:, :] += borrowed_ref[...]


def own(order, bounds, wanted, ctx, helped, stats, keyed, part, latents, borrowed, pred_weight):
    rows = part.shape[0]
    slots = ctx.shape[0]
    request_steps = slots // GATHERED
    first_help = slots // 2 // GATHERED
    whole = lambda *shape: pl.BlockSpec(shape, lambda i, o, c, w: (0,) * len(shape))
    chunk_of = pl.BlockSpec(
        (CHUNK, 256), lambda i, o, c, w: (jnp.maximum(i - request_steps, 0), 0)
    )
    return pl.pallas_call(
        own_kernel,
        grid_spec=pltpu.PrefetchScalarGridSpec(
            num_scalar_prefetch=3,
            grid=(request_steps + rows // CHUNK,),
            in_specs=[
                pl.BlockSpec(
                    (GATHERED, BLOCK, 256),
                    lambda i, o, c, w: (jnp.minimum(i, last_step(c[1], GATHERED)), 0, 0),
                ),
                pl.BlockSpec(
                    (GATHERED, BLOCK, 256),
                    lambda i, o, c, w: (
                        jnp.clip(i - first_help, 0, last_step(c[2] - slots // 2, GATHERED)), 0, 0
                    ),
                ),
                whole(slots, 2, 128),
                whole(rows, 256),
                chunk_of,
                chunk_of,
                whole(HALO, 256),
                whole(256, 256),
            ],
            out_specs=chunk_of,
            scratch_shapes=[pltpu.VMEM((rows, 256), F32)],
        ),
        out_shape=jax.ShapeDtypeStruct((rows, 256), F32),
        compiler_params=pltpu.CompilerParams(vmem_limit_bytes=VMEM),
        name="own",
    )(order, bounds, wanted, ctx, helped, stats, keyed, part, latents, borrowed, pred_weight)


def shifted(block, axis, distance):
    devices = range(lax.axis_size(axis))
    route = [(i - distance, i) for i in devices if i - distance in devices]
    return lax.ppermute(block, axis, route)


def swapped(block, axis):
    return lax.ppermute(block, axis, [(i, i ^ 1) for i in range(lax.axis_size(axis))])


def exchanged(slots):
    owners_count = slots.shape[0] // CAP
    sent = slots.reshape((owners_count, CAP) + slots.shape[1:])
    got = lax.all_to_all(sent, ("tm", "stream"), split_axis=0, concat_axis=0, tiled=True)
    return got.reshape(slots.shape)


def body(raw, starts, neg_owner, neg_block, enc_weight, tcn_weight, pred_weight):
    raw = raw[0]
    owners_count = lax.axis_size("tm") * lax.axis_size("stream")
    rim_starts = jnp.concatenate(
        [jnp.zeros((1, 128 - HALO), BF), starts[:, -HALO:].astype(BF)], axis=1
    )
    rim = shifted(jnp.concatenate([raw[:, -128:], rim_starts, rim_starts], axis=0), "tm", 1)
    half_weight = (tcn_weight * 0.5).astype(BF)
    tcn_back = jnp.swapaxes(tcn_weight, 2, 3)
    pred_back = pred_weight.T
    pack, push, slots, bd = prep(
        neg_owner[0].T, neg_block[0].T, raw, starts.reshape(-1, BLOCK), rim,
        enc_weight, owners_count,
    )
    pushed = exchanged(push)
    latents, ctx, slopes, levels, rim_slopes, rim_levels, keyed = forward(
        pack, bd, half_weight, pred_weight
    )
    pushed, ctx = lax.optimization_barrier((pushed, ctx))
    replies, order, bounds, wanted, extra = answer(pushed, pack)
    half = order.shape[0] // TOGETHER * TOGETHER // 2
    shared, replies = lax.optimization_barrier((swapped(extra, "tm"), replies))
    answers = exchanged(replies)
    request_ctx = recompute(order, bounds, pushed, bd, half_weight)
    shared, request_ctx = lax.optimization_barrier((shared, request_ctx))
    mate_count = shared[half, 0, 0].astype(jnp.int32)
    mate_bounds = jnp.stack([kept(mate_count, half) - half, mate_count - half])
    helped = swapped(
        recompute(
            lax.iota(jnp.int32, half), jnp.maximum(mate_bounds, 0), shared, bd, half_weight
        ),
        "tm",
    )
    answers, request_ctx = lax.optimization_barrier((answers, request_ctx))
    pred_grad, target_grad, stats = score(slots, answers, ctx, latents, levels, pred_weight, bd)
    got_stats = exchanged(stats)
    part, rim_grad = backward(
        pred_grad, slopes, levels, target_grad, rim_slopes, rim_levels, pred_back, tcn_back
    )
    borrowed = shifted(rim_grad, "tm", -1)
    return own(
        order, bounds, wanted, request_ctx, helped, got_stats, keyed, part, latents, borrowed, pred_weight
    )[None]


def solution(mesh):
    placed = (
        P("stream", None, "tm"),
        P("stream", "tm"),
        P("stream", "tm", None),
        P("stream", "tm", None),
        P(),
        P(),
        P(),
    )
    return jax.shard_map(
        body, mesh=mesh, in_specs=placed, out_specs=P("stream", "tm", None), check_vma=False
    )
```

profile of v0, /device:TPU:56, one launch (start us, length us, event | category | flops | bytes accessed | tf_op | source)
XLA Modules:
  0.0 238.9 jit_solution(15507136306060750800)
XLA Ops:
  0.0 0.7 slice.13
  0.7 0.7 slice_convert_fusion
  1.4 0.1 concatenate.6
  1.5 1.9 collective-permute-start
  3.4 5.1 %collective-permute-done.rim_ref = bf16[8,128]{1,0:T(8,128)(2,1)S(1)} collective-permute-done((bf16[8,128]{1,0:T(8,128)(2,1)S(1)}, bf16[8,128]{1,0:T(8,128)(2,1)S(1)}, u32[]{:S(2)}, u32[]{:S(2)}) %collective-permute-start) | collective-permute-done | bytes 2080 | tf_op jit(solution)/shard_map/ppermute | solution.py:688
  8.5 0.6 copy-done.6
  9.1 5.4 %prep.1 = (bf16[32,32,128]{2,1,0:T(8,128)(2,1)}, bf16[256,32,128]{2,1,0:T(8,128)(2,1)}, s32[128]{0:T(128)}, bf16[128,1024]{1,0:T(8,128)(2,1)}) custom-call(s32[4,32]{1,0:T(4,128)} %bitcast.32, s32[4,32]{1,0:T(4,128)} %bitcast.33, bf16[6,16384]{1,0:T(8,128)(2,1)} %bitcast.29, s32[32,128]{1,0:T(8,128)} %bitcast.31, bf16[8,128]{1,0:T(8,128)(2,1)} %copy-done.6, ...), custom_call_target="tpu_custom_call" | custom-call | tf_op jit(solution)/shard_map/prep/pallas_call | solution.py:145
  14.5 8.0 %all-to-all-start = ((bf16[128,2,32,128]{3,2,1,0:T(8,128)(2,1)}), bf16[128,2,32,128]{3,2,1,0:T(8,128)(2,1)S(1)}, u32[]{:S(2)}, u32[]{:S(2)}) async-start(bf16[128,2,32,128]{3,2,1,0:T(8,128)(2,1)} %bitcast.24), calls=%async_computation | async-start | bytes 4194304 | tf_op jit(solution)/shard_map/all_to_all | solution.py:698
  22.5 1.1 broadcast_multiply_fusion.w_ref
  23.6 20.3 %forward.1 = (bf16[4096,256]{1,0:T(8,128)(2,1)}, bf16[4096,256]{1,0:T(8,128)(2,1)}, bf16[4,4096,256]{2,1,0:T(8,128)(2,1)}, f32[4096,128]{1,0:T(8,128)}, bf16[4,3...) custom-call(bf16[32,32,128]{2,1,0:T(8,128)(2,1)} %get-tuple-element.35.pack_ref, ...), custom_call_target="tpu_custom_call" | custom-call | flops 5368709120 | bytes 18874368 | tf_op jit(solution)/shard_map/forward/pallas_call | solution.py:223
  44.0 6.3 %all-to-all-done = bf16[128,2,32,128]{3,2,1,0:T(8,128)(2,1)S(1)} async-done(((bf16[128,2,32,128]{3,2,1,0:T(8,128)(2,1)}), bf16[128,2,32,128]{3,2,1,0:T(8,128)(2,1)S(1)}, u32[]{:S(2)}, u32[]{:S(2)}) %all-to-all-start) | async-done | bytes 2097184 | tf_op jit(solution)/shard_map/all_to_all | solution.py:698
  50.3 1.3 copy-done
  51.6 6.4 %answer.1 = (bf16[256,32,128]{2,1,0:T(8,128)(2,1)}, s32[264]{0:T(512)}, s32[3]{0:T(128)}, s32[256]{0:T(256)}, bf16[129,32,128]{2,1,0:T(8,128)(2,1)}) custom-call(bf16[256,32,128]{2,1,0:T(8,128)(2,1)} %bitcast.21, bf16[32,32,128]{2,1,0:T(8,128)(2,1)} %get-tuple-element.35.pack_ref), custom_call_target="tpu_custom_call" | custom-call | tf_op jit(solution)/shard_map/answer/pallas_call | solution.py:302
  58.0 0.3 collective-permute-start.1
  58.3 51.1 %recompute.2.ctx_ref = bf16[256,128,256]{2,1,0:T(8,128)(2,1)} custom-call(s32[264]{0:T(512)} %get-tuple-element.39.order_ref, s32[3]{0:T(128)} %get-tuple-element.40.bounds_ref, bf16[256,32,128]{2,1,0:T(8,128)(2,1)} %bitcast.22, bf16[128,1024]{1,0:T(8,128)(2,1)} %get-tuple-element.36.bd_ref, bf16[4,2,256,256]{3,2,1,0:T(8,128)(2,1)} %broadcast_multiply_fusion.w_ref), custom_call_target="tpu_custom_call" | custom-call | flops 53687091200 | bytes 20971520 | tf_op jit(solution)/shard_map/recompute/pallas_call | solution.py:409
  109.4 0.6 slice.12
  110.6 0.6 add_maximum_fusion.bounds_ref
  111.2 0.5 iota.3.order_ref
  111.7 3.4 %recompute.3 = bf16[128,128,256]{2,1,0:T(8,128)(2,1)} custom-call(s32[128]{0:T(128)} %iota.3.order_ref, s32[2]{0:T(128)} %add_maximum_fusion.bounds_ref, bf16[129,32,128]{2,1,0:T(8,128)(2,1)} %copy-done.7, bf16[128,1024]{1,0:T(8,128)(2,1)} %get-tuple-element.36.bd_ref, bf16[4,2,256,256]{3,2,1,0:T(8,128)(2,1)} %broadcast_multiply_fusion.w_ref), custom_call_target="tpu_custom_call" | custom-call | flops 26843545600 | bytes 20971520 | tf_op jit(solution)/shard_map/recompute/pallas_call | solution.py:409
  115.1 22.9 %all-to-all-start.1 = ((bf16[128,2,32,128]{3,2,1,0:T(8,128)(2,1)}), bf16[128,2,32,128]{3,2,1,0:T(8,128)(2,1)S(1)}, u32[]{:S(2)}, u32[]{:S(2)}) async-start(bf16[128,2,32,128]{3,2,1,0:T(8,128)(2,1)} %bitcast.8), calls=%async_computation.1 | async-start | bytes 4194304 | tf_op jit(solution)/shard_map/all_to_all | solution.py:698
  138.0 1.3 copy.9
  139.4 0.7 copy.8
  140.1 25.7 %all-to-all-done.1 = bf16[128,2,32,128]{3,2,1,0:T(8,128)(2,1)S(1)} async-done(((bf16[128,2,32,128]{3,2,1,0:T(8,128)(2,1)}), bf16[128,2,32,128]{3,2,1,0:T(8,128)(2,1)S(1)}, u32[]{:S(2)}, u32[]{:S(2)}) %all-to-all-start.1) | async-done | bytes 2097184 | tf_op jit(solution)/shard_map/all_to_all | solution.py:698
  165.8 1.3 copy-done.2
  167.1 20.5 %score.1 = (bf16[4096,256]{1,0:T(8,128)(2,1)}, f32[4096,256]{1,0:T(8,128)}, f32[256,2,128]{2,1,0:T(2,128)}) custom-call(s32[128]{0:T(128)} %get-tuple-element.49.slot_ref, bf16[256,32,128]{2,1,0:T(8,128)(2,1)} %bitcast.25, bf16[4096,256]{1,0:T(8,128)(2,1)} %get-tuple-element.51.ctx_ref, bf16[4096,256]{1,0:T(8,128)(2,1)} %get-tuple-element.52.lat_ref, ...), custom_call_target="tpu_custom_call" | custom-call | flops 5368709120 | bytes 16777216 | tf_op jit(solution)/shard_map/score/pallas_call | solution.py:507
  187.6 6.6 %all-to-all-start.2 = ((f32[128,2,2,128]{3,2,1,0:T(2,128)}), f32[128,2,2,128]{3,2,1,0:T(2,128)S(1)}, u32[]{:S(2)}, u32[]{:S(2)}) async-start(f32[128,2,2,128]{3,2,1,0:T(2,128)} %bitcast.30), calls=%async_computation.2 | async-start | bytes 524288 | tf_op jit(solution)/shard_map/all_to_all | solution.py:698
  194.2 15.9 %backward.1 = (f32[4096,256]{1,0:T(8,128)}, f32[32,256]{1,0:T(8,128)}) custom-call(bf16[4096,256]{1,0:T(8,128)(2,1)} %get-tuple-element.56.pred_grad_ref, bf16[4,4096,256]{2,1,0:T(8,128)(2,1)} %get-tuple-element.57.slope_ref, f32[4096,128]{1,0:T(8,128)} %get-tuple-element.53.level_ref, f32[4096,256]{1,0:T(8,128)} %get-tuple-element.58.target_grad_ref, ...), custom_call_target="tpu_custom_call" | custom-call | flops 4831838208 | bytes 23068672 | tf_op jit(solution)/shard_map/backward/pallas_call | solution.py:572
  210.1 4.6 %collective-permute-start.3 = (f32[32,256]{1,0:T(8,128)}, f32[32,256]{1,0:T(8,128)S(1)}, u32[]{:S(2)}, u32[]{:S(2)}) collective-permute-start(f32[32,256]{1,0:T(8,128)} %get-tuple-element.62), channel_id=1, source_target_pairs={{4,0},{8,4},{12,8},{16,12},{20,16},{24,20},{28,24},{32,28},{36,32}... | collective-permute-start | bytes 98312 | tf_op jit(solution)/shard_map/ppermute | solution.py:688
  214.7 1.9 collective-permute-done.3.borrowed_ref
  216.6 0.6 copy-done.5
  217.2 0.1 copy-done.3
  217.3 21.5 %own.1 = f32[4096,256]{1,0:T(8,128)} custom-call(s32[264]{0:T(512)} %get-tuple-element.39.order_ref, s32[3]{0:T(128)} %get-tuple-element.40.bounds_ref, s32[256]{0:T(256)} %get-tuple-element.41.wanted_ref, bf16[256,128,256]{2,1,0:T(8,128)(2,1)} %recompute.2.ctx_ref, bf16[128,128,256]{2,1,0:T(8,128)(2,1)} %collective-permute-done.2.help_ref, ...), custom_call_target="tpu_custom_call" | custom-call | tf_op jit(solution)/shard_map/own/pallas_call | solution.py:653
  (16 shorter events, 0.0 us)
Async XLA Ops:
  1.5 7.0 %collective-permute-start = (bf16[8,128]{1,0:T(8,128)(2,1)S(1)}, bf16[8,128]{1,0:T(8,128)(2,1)S(1)}, u32[]{:S(2)}, u32[]{:S(2)}) collective-permute-start(bf16[8,128]{1,0:T(8,128)(2,1)S(1)} %pad_maximum_fusion), channel_id=1, source_target_pairs={{0,4},{4,8},{8,12},{12,16},{16,20},{20,24},{24,28},{28,32},{32,36}... | collective-permute-start | bytes 6152 | tf_op jit(solution)/shard_map/ppermute | solution.py:688
  8.5 0.6 copy-start.6
  14.5 8.0 %copy-start.1 = (bf16[4,2,256,256]{3,2,1,0:T(8,128)(2,1)S(1)}, bf16[4,2,256,256]{3,2,1,0:T(8,128)(2,1)}, u32[]{:S(2)}) copy-start(bf16[4,2,256,256]{3,2,1,0:T(8,128)(2,1)} %param.12) | copy-start | bytes 3145732
  14.5 35.8 %all-to-all-start = ((bf16[128,2,32,128]{3,2,1,0:T(8,128)(2,1)}), bf16[128,2,32,128]{3,2,1,0:T(8,128)(2,1)S(1)}, u32[]{:S(2)}, u32[]{:S(2)}) async-start(bf16[128,2,32,128]{3,2,1,0:T(8,128)(2,1)} %bitcast.24), calls=%async_computation | async-start | bytes 4194304 | tf_op jit(solution)/shard_map/all_to_all | solution.py:698
  50.3 1.3 copy-start
  58.0 51.3 %collective-permute-start.1 = (bf16[129,32,128]{2,1,0:T(8,128)(2,1)}, bf16[129,32,128]{2,1,0:T(8,128)(2,1)S(1)}, u32[]{:S(2)}, u32[]{:S(2)}) collective-permute-start(bf16[129,32,128]{2,1,0:T(8,128)(2,1)} %get-tuple-element.42), channel_id=1, source_target_pairs={{0,4},{4,0},{8,12},{12,8},{16,20},{20,16},{24,28},{28,24},{32,36},... | collective-permute-start | bytes 3170312 | tf_op jit(solution)/shard_map/ppermute | solution.py:692
  109.4 2.4 copy-start.7
  115.1 101.6 %collective-permute-start.2 = (bf16[128,128,256]{2,1,0:T(8,128)(2,1)}, bf16[128,128,256]{2,1,0:T(8,128)(2,1)}, u32[]{:S(2)}, u32[]{:S(2)}) collective-permute-start(bf16[128,128,256]{2,1,0:T(8,128)(2,1)} %recompute.3), channel_id=1, source_target_pairs={{0,4},{4,0},{8,12},{12,8},{16,20},{20,16},{24,28},{28,24},{32,36},... | collective-permute-start | bytes 25165832 | tf_op jit(solution)/shard_map/ppermute | solution.py:692
  115.1 50.7 %all-to-all-start.1 = ((bf16[128,2,32,128]{3,2,1,0:T(8,128)(2,1)}), bf16[128,2,32,128]{3,2,1,0:T(8,128)(2,1)S(1)}, u32[]{:S(2)}, u32[]{:S(2)}) async-start(bf16[128,2,32,128]{3,2,1,0:T(8,128)(2,1)} %bitcast.8), calls=%async_computation.1 | async-start | bytes 4194304 | tf_op jit(solution)/shard_map/all_to_all | solution.py:698
  138.0 1.3 copy-start.4
  165.8 1.3 copy-start.2
  187.6 29.0 %all-to-all-start.2 = ((f32[128,2,2,128]{3,2,1,0:T(2,128)}), f32[128,2,2,128]{3,2,1,0:T(2,128)S(1)}, u32[]{:S(2)}, u32[]{:S(2)}) async-start(f32[128,2,2,128]{3,2,1,0:T(2,128)} %bitcast.30), calls=%async_computation.2 | async-start | bytes 524288 | tf_op jit(solution)/shard_map/all_to_all | solution.py:698
  210.1 6.5 %collective-permute-start.3 = (f32[32,256]{1,0:T(8,128)}, f32[32,256]{1,0:T(8,128)S(1)}, u32[]{:S(2)}, u32[]{:S(2)}) collective-permute-start(f32[32,256]{1,0:T(8,128)} %get-tuple-element.62), channel_id=1, source_target_pairs={{4,0},{8,4},{12,8},{16,12},{20,16},{24,20},{28,24},{32,28},{36,32}... | collective-permute-start | bytes 98312 | tf_op jit(solution)/shard_map/ppermute | solution.py:688
  216.6 0.6 copy-start.5
  216.6 0.7 copy-start.3
where the time goes:
time: 240 us; the launch traced here: 239 us
  Pallas kernels  144 us (60%)
  starting transfers between devices  44.3 us (18%)
  waiting for transfers between devices  39 us (16%)
  local copies, waits for them, and re-layouts  7.86 us (3%)
  other arithmetic  2.44 us (1%)
    pallas_call x2, Pallas kernels, recompute(): pl.pallas_call(recompute_kernel, grid_spec=pltpu.PrefetchScalarGridSpec(n...  54.4 us
    all_to_all x3, starting transfers between devices, exchanged(): lax.all_to_all(sent, ('tm', 'stream'), split_axis=0, concat_axis=0, tiled...  37.5 us
    all_to_all x3, waiting for transfers between devices, exchanged(): lax.all_to_all(sent, ('tm', 'stream'), split_axis=0, concat_axis=0, tiled...  32 us
    pallas_call x1, Pallas kernels, own(): pl.pallas_call(own_kernel, grid_spec=pltpu.PrefetchScalarGridSpec(num_sca...  21.5 us
    pallas_call x1, Pallas kernels, score(): pl.pallas_call(score_kernel, grid_spec=pltpu.PrefetchScalarGridSpec(num_s...  20.5 us
    pallas_call x1, Pallas kernels, forward(): pl.pallas_call(forward_kernel, grid=(steps,), out_shape=(jax.ShapeDtypeSt...  20.3 us
    pallas_call x1, Pallas kernels, backward(): pl.pallas_call(backward_kernel, grid=(steps,), out_shape=(jax.ShapeDtypeS...  15.9 us
    ppermute x2, waiting for transfers between devices, shifted(): return lax.ppermute(block, axis, route)  6.98 us
  transfers between devices with their start and end apart: 7, of which 4 were waited for; matrix products, arithmetic and copies ran while one was open for 1% of the time, Pallas kernels for 45%

commit v1 on v0

--- a/solution.py
+++ b/solution.py
@@ -717,13 +717,15 @@
     latents, ctx, slopes, levels, rim_slopes, rim_levels, keyed = forward(
         pack, bd, half_weight, pred_weight
     )
-    pushed, ctx = lax.optimization_barrier((pushed, ctx))
+    pushed, ctx, tcn_back, pred_back = lax.optimization_barrier(
+        (pushed, ctx, tcn_back, pred_back)
+    )
     replies, order, bounds, wanted, extra = answer(pushed, pack)
     half = order.shape[0] // TOGETHER * TOGETHER // 2
-    shared, replies = lax.optimization_barrier((swapped(extra, "tm"), replies))
+    shared, replies, order = lax.optimization_barrier((swapped(extra, "tm"), replies, order))
     answers = exchanged(replies)
     request_ctx = recompute(order, bounds, pushed, bd, half_weight)
-    shared, request_ctx = lax.optimization_barrier((shared, request_ctx))
+    shared, request_ctx, answers = lax.optimization_barrier((shared, request_ctx, answers))
     mate_count = shared[half, 0, 0].astype(jnp.int32)
     mate_bounds = jnp.stack([kept(mate_count, half) - half, mate_count - half])
     helped = swapped(
@@ -732,7 +734,6 @@
         ),
         "tm",
     )
-    answers, request_ctx = lax.optimization_barrier((answers, request_ctx))
     pred_grad, target_grad, stats = score(slots, answers, ctx, latents, levels, pred_weight, bd)
     got_stats = exchanged(stats)
     part, rim_grad = backward(

time: 240 us -> 200 us (0.83)
  the two profiles are of different devices: /device:TPU:56 before, /device:TPU:88 now
where the time goes in v1:
time: 200 us; the launch traced here: 199 us
  Pallas kernels  144 us (72%)
  starting transfers between devices  33.1 us (17%)
  waiting for transfers between devices  11.8 us (6%)
  local copies, waits for them, and re-layouts  6.47 us (3%)
  other arithmetic  2.42 us (1%)
    pallas_call x2, Pallas kernels, recompute(): pl.pallas_call(recompute_kernel, grid_spec=pltpu.PrefetchScalarGridSpec(n...  54.4 us
    all_to_all x3, starting transfers between devices, exchanged(): lax.all_to_all(sent, ('tm', 'stream'), split_axis=0, concat_axis=0, tiled...  26.5 us
    pallas_call x1, Pallas kernels, own(): pl.pallas_call(own_kernel, grid_spec=pltpu.PrefetchScalarGridSpec(num_sca...  21.5 us
    pallas_call x1, Pallas kernels, score(): pl.pallas_call(score_kernel, grid_spec=pltpu.PrefetchScalarGridSpec(num_s...  20.5 us
    pallas_call x1, Pallas kernels, forward(): pl.pallas_call(forward_kernel, grid=(steps,), out_shape=(jax.ShapeDtypeSt...  20.4 us
    pallas_call x1, Pallas kernels, backward(): pl.pallas_call(backward_kernel, grid=(steps,), out_shape=(jax.ShapeDtypeS...  15.9 us
    ppermute x2, waiting for transfers between devices, shifted(): return lax.ppermute(block, axis, route)  6.98 us
    ppermute x2, starting transfers between devices, shifted(): return lax.ppermute(block, axis, route)  6.52 us
  transfers between devices with their start and end apart: 7, of which 4 were waited for; matrix products, arithmetic and copies ran while one was open for 2% of the time, Pallas kernels for 54%

profile of v1, /device:TPU:88, one launch (start us, length us, event | category | flops | bytes accessed | tf_op | source)
XLA Modules:
  0.0 199.0 jit_solution(18233050882338938880)
XLA Ops:
  0.0 0.7 slice.13
  0.7 0.7 slice_convert_fusion
  1.4 0.1 concatenate.6
  1.5 1.9 collective-permute-start
  3.4 5.1 %collective-permute-done.rim_ref = bf16[8,128]{1,0:T(8,128)(2,1)S(1)} collective-permute-done((bf16[8,128]{1,0:T(8,128)(2,1)S(1)}, bf16[8,128]{1,0:T(8,128)(2,1)S(1)}, u32[]{:S(2)}, u32[]{:S(2)}) %collective-permute-start) | collective-permute-done | bytes 2080 | tf_op jit(solution)/shard_map/ppermute | solution.py:688
  8.5 0.5 copy-done.6
  9.0 5.4 %prep.1 = (bf16[32,32,128]{2,1,0:T(8,128)(2,1)}, bf16[256,32,128]{2,1,0:T(8,128)(2,1)}, s32[128]{0:T(128)}, bf16[128,1024]{1,0:T(8,128)(2,1)}) custom-call(s32[4,32]{1,0:T(4,128)} %bitcast.33, s32[4,32]{1,0:T(4,128)} %bitcast.34, bf16[6,16384]{1,0:T(8,128)(2,1)} %bitcast.30, s32[32,128]{1,0:T(8,128)} %bitcast.32, bf16[8,128]{1,0:T(8,128)(2,1)} %copy-done.6, ...), custom_call_target="tpu_custom_call" | custom-call | tf_op jit(solution)/shard_map/prep/pallas_call | solution.py:145
  14.5 0.0 copy-start.1
  14.5 7.8 %all-to-all-start = ((bf16[128,2,32,128]{3,2,1,0:T(8,128)(2,1)}), bf16[128,2,32,128]{3,2,1,0:T(8,128)(2,1)S(1)}, u32[]{:S(2)}, u32[]{:S(2)}) async-start(bf16[128,2,32,128]{3,2,1,0:T(8,128)(2,1)} %bitcast.25), calls=%async_computation | async-start | bytes 4194304 | tf_op jit(solution)/shard_map/all_to_all | solution.py:698
  22.3 1.3 copy.8
  23.6 0.7 copy.9
  24.4 1.1 broadcast_multiply_fusion.w_ref
  25.5 20.4 %forward.1 = (bf16[4096,256]{1,0:T(8,128)(2,1)}, bf16[4096,256]{1,0:T(8,128)(2,1)}, bf16[4,4096,256]{2,1,0:T(8,128)(2,1)}, f32[4096,128]{1,0:T(8,128)}, bf16[4,3...) custom-call(bf16[32,32,128]{2,1,0:T(8,128)(2,1)} %get-tuple-element.37.pack_ref, ...), custom_call_target="tpu_custom_call" | custom-call | flops 5368709120 | bytes 18874368 | tf_op jit(solution)/shard_map/forward/pallas_call | solution.py:223
  45.8 1.9 all-to-all-done
  47.8 1.3 copy-done
  49.1 6.3 %answer.1 = (bf16[256,32,128]{2,1,0:T(8,128)(2,1)}, s32[264]{0:T(512)}, s32[3]{0:T(128)}, s32[256]{0:T(256)}, bf16[129,32,128]{2,1,0:T(8,128)(2,1)}) custom-call(bf16[256,32,128]{2,1,0:T(8,128)(2,1)} %bitcast.21, bf16[32,32,128]{2,1,0:T(8,128)(2,1)} %get-tuple-element.37.pack_ref), custom_call_target="tpu_custom_call" | custom-call | tf_op jit(solution)/shard_map/answer/pallas_call | solution.py:302
  55.3 0.1 collective-permute-start.1
  55.4 2.9 %collective-permute-done.1.push_ref = bf16[129,32,128]{2,1,0:T(8,128)(2,1)S(1)} collective-permute-done((bf16[129,32,128]{2,1,0:T(8,128)(2,1)}, bf16[129,32,128]{2,1,0:T(8,128)(2,1)S(1)}, u32[]{:S(2)}, u32[]{:S(2)}) %collective-permute-start.1) | collective-permute-done | bytes 1056800 | tf_op jit(solution)/shard_map/ppermute | solution.py:692
  58.3 8.8 %all-to-all-start.1 = ((bf16[128,2,32,128]{3,2,1,0:T(8,128)(2,1)}), bf16[128,2,32,128]{3,2,1,0:T(8,128)(2,1)S(1)}, u32[]{:S(2)}, u32[]{:S(2)}) async-start(bf16[128,2,32,128]{3,2,1,0:T(8,128)(2,1)} %bitcast.26), calls=%async_computation.1 | async-start | bytes 4194304 | tf_op jit(solution)/shard_map/all_to_all | solution.py:698
  67.1 51.1 %recompute.2.ctx_ref = bf16[256,128,256]{2,1,0:T(8,128)(2,1)} custom-call(s32[264]{0:T(512)} %get-tuple-element.44.order_ref, s32[3]{0:T(128)} %get-tuple-element.45.bounds_ref, bf16[256,32,128]{2,1,0:T(8,128)(2,1)} %bitcast.22, bf16[128,1024]{1,0:T(8,128)(2,1)} %get-tuple-element.38.bd_ref, bf16[4,2,256,256]{3,2,1,0:T(8,128)(2,1)} %broadcast_multiply_fusion.w_ref), custom_call_target="tpu_custom_call" | custom-call | flops 53687091200 | bytes 20971520 | tf_op jit(solution)/shard_map/recompute/pallas_call | solution.py:409
  118.2 0.5 slice.12
  119.4 0.6 add_maximum_fusion.bounds_ref
  120.1 0.5 iota.3.order_ref
  120.6 3.4 %recompute.3 = bf16[128,128,256]{2,1,0:T(8,128)(2,1)} custom-call(s32[128]{0:T(128)} %iota.3.order_ref, s32[2]{0:T(128)} %add_maximum_fusion.bounds_ref, bf16[129,32,128]{2,1,0:T(8,128)(2,1)} %copy-done.7, bf16[128,1024]{1,0:T(8,128)(2,1)} %get-tuple-element.38.bd_ref, bf16[4,2,256,256]{3,2,1,0:T(8,128)(2,1)} %broadcast_multiply_fusion.w_ref), custom_call_target="tpu_custom_call" | custom-call | flops 26843545600 | bytes 20971520 | tf_op jit(solution)/shard_map/recompute/pallas_call | solution.py:409
  123.9 20.5 %score.1 = (bf16[4096,256]{1,0:T(8,128)(2,1)}, f32[4096,256]{1,0:T(8,128)}, f32[256,2,128]{2,1,0:T(2,128)}) custom-call(s32[128]{0:T(128)} %get-tuple-element.51.slot_ref, bf16[256,32,128]{2,1,0:T(8,128)(2,1)} %bitcast.24, bf16[4096,256]{1,0:T(8,128)(2,1)} %get-tuple-element.53.ctx_ref, bf16[4096,256]{1,0:T(8,128)(2,1)} %get-tuple-element.54.lat_ref, ...), custom_call_target="tpu_custom_call" | custom-call | flops 5368709120 | bytes 16777216 | tf_op jit(solution)/shard_map/score/pallas_call | solution.py:507
  144.4 9.9 %all-to-all-start.2 = ((f32[128,2,2,128]{3,2,1,0:T(2,128)}), f32[128,2,2,128]{3,2,1,0:T(2,128)S(1)}, u32[]{:S(2)}, u32[]{:S(2)}) async-start(f32[128,2,2,128]{3,2,1,0:T(2,128)} %bitcast.31), calls=%async_computation.2 | async-start | bytes 524288 | tf_op jit(solution)/shard_map/all_to_all | solution.py:698
  154.4 15.9 %backward.1 = (f32[4096,256]{1,0:T(8,128)}, f32[32,256]{1,0:T(8,128)}) custom-call(bf16[4096,256]{1,0:T(8,128)(2,1)} %get-tuple-element.58.pred_grad_ref, bf16[4,4096,256]{2,1,0:T(8,128)(2,1)} %get-tuple-element.59.slope_ref, f32[4096,128]{1,0:T(8,128)} %get-tuple-element.55.level_ref, f32[4096,256]{1,0:T(8,128)} %get-tuple-element.60.target_grad_ref, ...), custom_call_target="tpu_custom_call" | custom-call | flops 4831838208 | bytes 23068672 | tf_op jit(solution)/shard_map/backward/pallas_call | solution.py:572
  170.2 4.6 %collective-permute-start.3 = (f32[32,256]{1,0:T(8,128)}, f32[32,256]{1,0:T(8,128)S(1)}, u32[]{:S(2)}, u32[]{:S(2)}) collective-permute-start(f32[32,256]{1,0:T(8,128)} %get-tuple-element.66), channel_id=1, source_target_pairs={{4,0},{8,4},{12,8},{16,12},{20,16},{24,20},{28,24},{32,28},{36,32}... | collective-permute-start | bytes 98312 | tf_op jit(solution)/shard_map/ppermute | solution.py:688
  174.9 1.9 collective-permute-done.3.borrowed_ref
  176.8 0.6 copy-done.5
  177.4 0.1 copy-done.3
  177.5 21.5 %own.1 = f32[4096,256]{1,0:T(8,128)} custom-call(s32[264]{0:T(512)} %get-tuple-element.44.order_ref, s32[3]{0:T(128)} %get-tuple-element.45.bounds_ref, s32[256]{0:T(256)} %get-tuple-element.46.wanted_ref, bf16[256,128,256]{2,1,0:T(8,128)(2,1)} %recompute.2.ctx_ref, bf16[128,128,256]{2,1,0:T(8,128)(2,1)} %collective-permute-done.2.help_ref, ...), custom_call_target="tpu_custom_call" | custom-call | tf_op jit(solution)/shard_map/own/pallas_call | solution.py:653
  (16 shorter events, 0.0 us)
Async XLA Ops:
  1.5 7.0 %collective-permute-start = (bf16[8,128]{1,0:T(8,128)(2,1)S(1)}, bf16[8,128]{1,0:T(8,128)(2,1)S(1)}, u32[]{:S(2)}, u32[]{:S(2)}) collective-permute-start(bf16[8,128]{1,0:T(8,128)(2,1)S(1)} %pad_maximum_fusion), channel_id=1, source_target_pairs={{0,4},{4,8},{8,12},{12,16},{16,20},{20,24},{24,28},{28,32},{32,36}... | collective-permute-start | bytes 6152 | tf_op jit(solution)/shard_map/ppermute | solution.py:688
  8.5 0.5 copy-start.6
  14.5 7.8 %copy-start.1 = (bf16[4,2,256,256]{3,2,1,0:T(8,128)(2,1)S(1)}, bf16[4,2,256,256]{3,2,1,0:T(8,128)(2,1)}, u32[]{:S(2)}) copy-start(bf16[4,2,256,256]{3,2,1,0:T(8,128)(2,1)} %param.12) | copy-start | bytes 3145732
  14.5 9.2 %copy-start.4 = (bf16[256,256]{1,0:T(8,128)(2,1)S(1)}, bf16[256,256]{1,0:T(8,128)(2,1)}, u32[]{:S(2)}) copy-start(bf16[256,256]{1,0:T(8,128)(2,1)} %pred_ref.5) | copy-start | bytes 393220
  14.5 33.3 %all-to-all-start = ((bf16[128,2,32,128]{3,2,1,0:T(8,128)(2,1)}), bf16[128,2,32,128]{3,2,1,0:T(8,128)(2,1)S(1)}, u32[]{:S(2)}, u32[]{:S(2)}) async-start(bf16[128,2,32,128]{3,2,1,0:T(8,128)(2,1)} %bitcast.25), calls=%async_computation | async-start | bytes 4194304 | tf_op jit(solution)/shard_map/all_to_all | solution.py:698
  47.8 1.3 copy-start
  55.3 3.0 %collective-permute-start.1 = (bf16[129,32,128]{2,1,0:T(8,128)(2,1)}, bf16[129,32,128]{2,1,0:T(8,128)(2,1)S(1)}, u32[]{:S(2)}, u32[]{:S(2)}) collective-permute-start(bf16[129,32,128]{2,1,0:T(8,128)(2,1)} %get-tuple-element.41), channel_id=1, source_target_pairs={{0,4},{4,0},{8,12},{12,8},{16,20},{20,16},{24,28},{28,24},{32,36},... | collective-permute-start | bytes 3170312 | tf_op jit(solution)/shard_map/ppermute | solution.py:692
  58.3 59.9 %copy-start.7 = (bf16[129,32,128]{2,1,0:T(8,128)(2,1)}, bf16[129,32,128]{2,1,0:T(8,128)(2,1)S(1)}, u32[]{:S(2)}) copy-start(bf16[129,32,128]{2,1,0:T(8,128)(2,1)S(1)} %collective-permute-done.1.push_ref) | copy-start | bytes 3170308
  58.3 59.9 %all-to-all-start.1 = ((bf16[128,2,32,128]{3,2,1,0:T(8,128)(2,1)}), bf16[128,2,32,128]{3,2,1,0:T(8,128)(2,1)S(1)}, u32[]{:S(2)}, u32[]{:S(2)}) async-start(bf16[128,2,32,128]{3,2,1,0:T(8,128)(2,1)} %bitcast.26), calls=%async_computation.1 | async-start | bytes 4194304 | tf_op jit(solution)/shard_map/all_to_all | solution.py:698
  118.2 5.7 %copy-start.2 = (bf16[128,2,32,128]{3,2,1,0:T(8,128)(2,1)}, bf16[128,2,32,128]{3,2,1,0:T(8,128)(2,1)S(1)}, u32[]{:S(2)}) copy-start(bf16[128,2,32,128]{3,2,1,0:T(8,128)(2,1)S(1)} %all-to-all-done.1) | copy-start | bytes 6291460
  123.9 52.8 %collective-permute-start.2 = (bf16[128,128,256]{2,1,0:T(8,128)(2,1)}, bf16[128,128,256]{2,1,0:T(8,128)(2,1)}, u32[]{:S(2)}, u32[]{:S(2)}) collective-permute-start(bf16[128,128,256]{2,1,0:T(8,128)(2,1)} %recompute.3), channel_id=1, source_target_pairs={{0,4},{4,0},{8,12},{12,8},{16,20},{20,16},{24,28},{28,24},{32,36},... | collective-permute-start | bytes 25165832 | tf_op jit(solution)/shard_map/ppermute | solution.py:692
  144.4 32.4 %all-to-all-start.2 = ((f32[128,2,2,128]{3,2,1,0:T(2,128)}), f32[128,2,2,128]{3,2,1,0:T(2,128)S(1)}, u32[]{:S(2)}, u32[]{:S(2)}) async-start(f32[128,2,2,128]{3,2,1,0:T(2,128)} %bitcast.31), calls=%async_computation.2 | async-start | bytes 524288 | tf_op jit(solution)/shard_map/all_to_all | solution.py:698
  170.2 6.5 %collective-permute-start.3 = (f32[32,256]{1,0:T(8,128)}, f32[32,256]{1,0:T(8,128)S(1)}, u32[]{:S(2)}, u32[]{:S(2)}) collective-permute-start(f32[32,256]{1,0:T(8,128)} %get-tuple-element.66), channel_id=1, source_target_pairs={{4,0},{8,4},{12,8},{16,12},{20,16},{24,20},{28,24},{32,28},{36,32}... | collective-permute-start | bytes 98312 | tf_op jit(solution)/shard_map/ppermute | solution.py:688
  176.7 0.6 copy-start.5
  176.8 0.7 copy-start.3

commit v2 on v1

--- a/solution.py
+++ b/solution.py
@@ -13,7 +13,7 @@
 LAYERS = 4
 PACK = 32
 TOGETHER = 16
-PAIRED = 1
+PAIRED = 2
 PIECES = 4
 SKEW = 1
 GATHERED = 64
@@ -21,7 +21,8 @@
 NOTE = 95
 LEAD = 20
 SEGMENT = 512
-SCORED = 4
+SCORED = 8
+SPAN = 1024
 SCALE = 10.0
 EPSILON = 1e-06
 BF = jnp.bfloat16
@@ -566,9 +567,9 @@
 
 def backward(pred_grad, slopes, levels, target_grad, rim_slopes, rim_levels, pred_weight, weight):
     rows = pred_grad.shape[0]
-    steps = rows // SEGMENT
+    steps = rows // SPAN
     whole = lambda *shape: pl.BlockSpec(shape, lambda i: (0,) * len(shape))
-    rows_of = lambda width: pl.BlockSpec((SEGMENT, width), lambda i: (steps - 1 - i, 0))
+    rows_of = lambda width: pl.BlockSpec((SPAN, width), lambda i: (steps - 1 - i, 0))
     return pl.pallas_call(
         backward_kernel,
         grid=(steps,),
@@ -578,7 +579,7 @@
         ),
         in_specs=[
             rows_of(256),
-            pl.BlockSpec((LAYERS, SEGMENT, 256), lambda i: (0, steps - 1 - i, 0)),
+            pl.BlockSpec((LAYERS, SPAN, 256), lambda i: (0, steps - 1 - i, 0)),
             rows_of(128),
             rows_of(256),
             whole(LAYERS, HALO, 256),

time: 200 us -> 213 us (1.065)
  the two profiles are of different devices: /device:TPU:88 before, /device:TPU:35 now
where the time goes in v2:
time: 213 us
  Pallas kernels  145 us (68%)
  starting transfers between devices  46.9 us (22%)
  waiting for transfers between devices  10.5 us (5%)
  local copies, waits for them, and re-layouts  6.47 us (3%)
  other arithmetic  2.42 us (1%)
    pallas_call x2, Pallas kernels, recompute(): pl.pallas_call(recompute_kernel, grid_spec=pltpu.PrefetchScalarGridSpec(n...  56.6 us
    all_to_all x3, starting transfers between devices, exchanged(): lax.all_to_all(sent, ('tm', 'stream'), split_axis=0, concat_axis=0, tiled...  39.2 us
    pallas_call x1, Pallas kernels, own(): pl.pallas_call(own_kernel, grid_spec=pltpu.PrefetchScalarGridSpec(num_sca...  21.5 us
    pallas_call x1, Pallas kernels, score(): pl.pallas_call(score_kernel, grid_spec=pltpu.PrefetchScalarGridSpec(num_s...  20.5 us
    pallas_call x1, Pallas kernels, forward(): pl.pallas_call(forward_kernel, grid=(steps,), out_shape=(jax.ShapeDtypeSt...  20.3 us
    pallas_call x1, Pallas kernels, backward(): pl.pallas_call(backward_kernel, grid=(steps,), out_shape=(jax.ShapeDtypeS...  14.8 us
    pallas_call x1, Pallas kernels, answer(): pl.pallas_call(answer_kernel, out_shape=(jax.ShapeDtypeStruct((slots, PAC...  6.25 us
    ppermute x2, starting transfers between devices, shifted(): return lax.ppermute(block, axis, route)  5.94 us
  transfers between devices with their start and end apart: 7, of which 4 were waited for; matrix products, arithmetic and copies ran while one was open for 1% of the time, Pallas kernels for 51%

profile of v2, /device:TPU:35, one launch (start us, length us, event | category | flops | bytes accessed | tf_op | source)
XLA Modules:
  0.0 212.6 jit_solution(2217599873235552925)
XLA Ops:
  0.0 0.7 slice.13
  0.7 0.7 slice_convert_fusion
  1.4 0.1 concatenate.6
  1.5 3.7 %collective-permute-start = (bf16[8,128]{1,0:T(8,128)(2,1)S(1)}, bf16[8,128]{1,0:T(8,128)(2,1)S(1)}, u32[]{:S(2)}, u32[]{:S(2)}) collective-permute-start(bf16[8,128]{1,0:T(8,128)(2,1)S(1)} %pad_maximum_fusion), channel_id=1, source_target_pairs={{0,4},{4,8},{8,12},{12,16},{16,20},{20,24},{24,28},{28,32},{32,36}... | collective-permute-start | bytes 6152 | tf_op jit(solution)/shard_map/ppermute | solution.py:689
  5.2 0.7 collective-permute-done.rim_ref
  5.9 0.5 copy-done.6
  6.4 5.4 %prep.1 = (bf16[32,32,128]{2,1,0:T(8,128)(2,1)}, bf16[256,32,128]{2,1,0:T(8,128)(2,1)}, s32[128]{0:T(128)}, bf16[128,1024]{1,0:T(8,128)(2,1)}) custom-call(s32[4,32]{1,0:T(4,128)} %bitcast.33, s32[4,32]{1,0:T(4,128)} %bitcast.34, bf16[6,16384]{1,0:T(8,128)(2,1)} %bitcast.30, s32[32,128]{1,0:T(8,128)} %bitcast.32, bf16[8,128]{1,0:T(8,128)(2,1)} %copy-done.6, ...), custom_call_target="tpu_custom_call" | custom-call | tf_op jit(solution)/shard_map/prep/pallas_call | solution.py:146
  11.9 11.0 %all-to-all-start = ((bf16[128,2,32,128]{3,2,1,0:T(8,128)(2,1)}), bf16[128,2,32,128]{3,2,1,0:T(8,128)(2,1)S(1)}, u32[]{:S(2)}, u32[]{:S(2)}) async-start(bf16[128,2,32,128]{3,2,1,0:T(8,128)(2,1)} %bitcast.25), calls=%async_computation | async-start | bytes 4194304 | tf_op jit(solution)/shard_map/all_to_all | solution.py:699
  22.9 1.3 copy.8
  24.3 0.7 copy.9
  25.0 1.1 broadcast_multiply_fusion.w_ref
  26.1 20.3 %forward.1 = (bf16[4096,256]{1,0:T(8,128)(2,1)}, bf16[4096,256]{1,0:T(8,128)(2,1)}, bf16[4,4096,256]{2,1,0:T(8,128)(2,1)}, f32[4096,128]{1,0:T(8,128)}, bf16[4,3...) custom-call(bf16[32,32,128]{2,1,0:T(8,128)(2,1)} %get-tuple-element.37.pack_ref, ...), custom_call_target="tpu_custom_call" | custom-call | flops 5368709120 | bytes 18874368 | tf_op jit(solution)/shard_map/forward/pallas_call | solution.py:224
  46.4 4.1 %all-to-all-done = bf16[128,2,32,128]{3,2,1,0:T(8,128)(2,1)S(1)} async-done(((bf16[128,2,32,128]{3,2,1,0:T(8,128)(2,1)}), bf16[128,2,32,128]{3,2,1,0:T(8,128)(2,1)S(1)}, u32[]{:S(2)}, u32[]{:S(2)}) %all-to-all-start) | async-done | bytes 2097184 | tf_op jit(solution)/shard_map/all_to_all | solution.py:699
  50.6 1.3 copy-done
  51.9 6.3 %answer.1 = (bf16[256,32,128]{2,1,0:T(8,128)(2,1)}, s32[264]{0:T(512)}, s32[3]{0:T(128)}, s32[256]{0:T(256)}, bf16[129,32,128]{2,1,0:T(8,128)(2,1)}) custom-call(bf16[256,32,128]{2,1,0:T(8,128)(2,1)} %bitcast.21, bf16[32,32,128]{2,1,0:T(8,128)(2,1)} %get-tuple-element.37.pack_ref), custom_call_target="tpu_custom_call" | custom-call | tf_op jit(solution)/shard_map/answer/pallas_call | solution.py:303
  58.1 1.1 collective-permute-start.1
  59.2 2.5 %collective-permute-done.1.push_ref = bf16[129,32,128]{2,1,0:T(8,128)(2,1)S(1)} collective-permute-done((bf16[129,32,128]{2,1,0:T(8,128)(2,1)}, bf16[129,32,128]{2,1,0:T(8,128)(2,1)S(1)}, u32[]{:S(2)}, u32[]{:S(2)}) %collective-permute-start.1) | collective-permute-done | bytes 1056800 | tf_op jit(solution)/shard_map/ppermute | solution.py:693
  61.7 5.5 %all-to-all-start.1 = ((bf16[128,2,32,128]{3,2,1,0:T(8,128)(2,1)}), bf16[128,2,32,128]{3,2,1,0:T(8,128)(2,1)S(1)}, u32[]{:S(2)}, u32[]{:S(2)}) async-start(bf16[128,2,32,128]{3,2,1,0:T(8,128)(2,1)} %bitcast.26), calls=%async_computation.1 | async-start | bytes 4194304 | tf_op jit(solution)/shard_map/all_to_all | solution.py:699
  67.2 52.8 %recompute.2.ctx_ref = bf16[256,128,256]{2,1,0:T(8,128)(2,1)} custom-call(s32[264]{0:T(512)} %get-tuple-element.44.order_ref, s32[3]{0:T(128)} %get-tuple-element.45.bounds_ref, bf16[256,32,128]{2,1,0:T(8,128)(2,1)} %bitcast.22, bf16[128,1024]{1,0:T(8,128)(2,1)} %get-tuple-element.38.bd_ref, bf16[4,2,256,256]{3,2,1,0:T(8,128)(2,1)} %broadcast_multiply_fusion.w_ref), custom_call_target="tpu_custom_call" | custom-call | flops 53687091200 | bytes 20971520 | tf_op jit(solution)/shard_map/recompute/pallas_call | solution.py:410
  120.0 0.5 slice.12
  121.3 0.6 add_maximum_fusion.bounds_ref
  121.9 0.5 iota.3.order_ref
  122.4 3.9 %recompute.3 = bf16[128,128,256]{2,1,0:T(8,128)(2,1)} custom-call(s32[128]{0:T(128)} %iota.3.order_ref, s32[2]{0:T(128)} %add_maximum_fusion.bounds_ref, bf16[129,32,128]{2,1,0:T(8,128)(2,1)} %copy-done.7, bf16[128,1024]{1,0:T(8,128)(2,1)} %get-tuple-element.38.bd_ref, bf16[4,2,256,256]{3,2,1,0:T(8,128)(2,1)} %broadcast_multiply_fusion.w_ref), custom_call_target="tpu_custom_call" | custom-call | flops 26843545600 | bytes 20971520 | tf_op jit(solution)/shard_map/recompute/pallas_call | solution.py:410
  126.3 0.6 collective-permute-start.2
  126.9 20.5 %score.1 = (bf16[4096,256]{1,0:T(8,128)(2,1)}, f32[4096,256]{1,0:T(8,128)}, f32[256,2,128]{2,1,0:T(2,128)}) custom-call(s32[128]{0:T(128)} %get-tuple-element.51.slot_ref, bf16[256,32,128]{2,1,0:T(8,128)(2,1)} %bitcast.24, bf16[4096,256]{1,0:T(8,128)(2,1)} %get-tuple-element.53.ctx_ref, bf16[4096,256]{1,0:T(8,128)(2,1)} %get-tuple-element.54.lat_ref, ...), custom_call_target="tpu_custom_call" | custom-call | flops 5368709120 | bytes 16777216 | tf_op jit(solution)/shard_map/score/pallas_call | solution.py:508
  147.4 22.7 %all-to-all-start.2 = ((f32[128,2,2,128]{3,2,1,0:T(2,128)}), f32[128,2,2,128]{3,2,1,0:T(2,128)S(1)}, u32[]{:S(2)}, u32[]{:S(2)}) async-start(f32[128,2,2,128]{3,2,1,0:T(2,128)} %bitcast.31), calls=%async_computation.2 | async-start | bytes 524288 | tf_op jit(solution)/shard_map/all_to_all | solution.py:699
  170.1 14.8 %backward.1 = (f32[4096,256]{1,0:T(8,128)}, f32[32,256]{1,0:T(8,128)}) custom-call(bf16[4096,256]{1,0:T(8,128)(2,1)} %get-tuple-element.58.pred_grad_ref, bf16[4,4096,256]{2,1,0:T(8,128)(2,1)} %get-tuple-element.59.slope_ref, f32[4096,128]{1,0:T(8,128)} %get-tuple-element.55.level_ref, f32[4096,256]{1,0:T(8,128)} %get-tuple-element.60.target_grad_ref, ...), custom_call_target="tpu_custom_call" | custom-call | flops 4831838208 | bytes 23068672 | tf_op jit(solution)/shard_map/backward/pallas_call | solution.py:573
  184.9 2.3 %collective-permute-start.3 = (f32[32,256]{1,0:T(8,128)}, f32[32,256]{1,0:T(8,128)S(1)}, u32[]{:S(2)}, u32[]{:S(2)}) collective-permute-start(f32[32,256]{1,0:T(8,128)} %get-tuple-element.66), channel_id=1, source_target_pairs={{4,0},{8,4},{12,8},{16,12},{20,16},{24,20},{28,24},{32,28},{36,32}... | collective-permute-start | bytes 98312 | tf_op jit(solution)/shard_map/ppermute | solution.py:689
  187.2 3.2 %collective-permute-done.3.borrowed_ref = f32[32,256]{1,0:T(8,128)S(1)} collective-permute-done((f32[32,256]{1,0:T(8,128)}, f32[32,256]{1,0:T(8,128)S(1)}, u32[]{:S(2)}, u32[]{:S(2)}) %collective-permute-start.3) | collective-permute-done | bytes 32800 | tf_op jit(solution)/shard_map/ppermute | solution.py:689
  190.3 0.6 copy-done.5
  190.9 0.1 copy-done.3
  191.0 21.5 %own.1 = f32[4096,256]{1,0:T(8,128)} custom-call(s32[264]{0:T(512)} %get-tuple-element.44.order_ref, s32[3]{0:T(128)} %get-tuple-element.45.bounds_ref, s32[256]{0:T(256)} %get-tuple-element.46.wanted_ref, bf16[256,128,256]{2,1,0:T(8,128)(2,1)} %recompute.2.ctx_ref, bf16[128,128,256]{2,1,0:T(8,128)(2,1)} %collective-permute-done.2.help_ref, ...), custom_call_target="tpu_custom_call" | custom-call | tf_op jit(solution)/shard_map/own/pallas_call | solution.py:654
  (16 shorter events, 0.0 us)
Async XLA Ops:
  1.5 4.4 %collective-permute-start = (bf16[8,128]{1,0:T(8,128)(2,1)S(1)}, bf16[8,128]{1,0:T(8,128)(2,1)S(1)}, u32[]{:S(2)}, u32[]{:S(2)}) collective-permute-start(bf16[8,128]{1,0:T(8,128)(2,1)S(1)} %pad_maximum_fusion), channel_id=1, source_target_pairs={{0,4},{4,8},{8,12},{12,16},{16,20},{20,24},{24,28},{28,32},{32,36}... | collective-permute-start | bytes 6152 | tf_op jit(solution)/shard_map/ppermute | solution.py:689
  5.9 0.5 copy-start.6
  11.9 11.1 %copy-start.1 = (bf16[4,2,256,256]{3,2,1,0:T(8,128)(2,1)S(1)}, bf16[4,2,256,256]{3,2,1,0:T(8,128)(2,1)}, u32[]{:S(2)}) copy-start(bf16[4,2,256,256]{3,2,1,0:T(8,128)(2,1)} %param.12) | copy-start | bytes 3145732
  11.9 12.4 %copy-start.4 = (bf16[256,256]{1,0:T(8,128)(2,1)S(1)}, bf16[256,256]{1,0:T(8,128)(2,1)}, u32[]{:S(2)}) copy-start(bf16[256,256]{1,0:T(8,128)(2,1)} %pred_ref.5) | copy-start | bytes 393220
  11.9 38.7 %all-to-all-start = ((bf16[128,2,32,128]{3,2,1,0:T(8,128)(2,1)}), bf16[128,2,32,128]{3,2,1,0:T(8,128)(2,1)S(1)}, u32[]{:S(2)}, u32[]{:S(2)}) async-start(bf16[128,2,32,128]{3,2,1,0:T(8,128)(2,1)} %bitcast.25), calls=%async_computation | async-start | bytes 4194304 | tf_op jit(solution)/shard_map/all_to_all | solution.py:699
  50.6 1.3 copy-start
  58.1 3.6 %collective-permute-start.1 = (bf16[129,32,128]{2,1,0:T(8,128)(2,1)}, bf16[129,32,128]{2,1,0:T(8,128)(2,1)S(1)}, u32[]{:S(2)}, u32[]{:S(2)}) collective-permute-start(bf16[129,32,128]{2,1,0:T(8,128)(2,1)} %get-tuple-element.41), channel_id=1, source_target_pairs={{0,4},{4,0},{8,12},{12,8},{16,20},{20,16},{24,28},{28,24},{32,36},... | collective-permute-start | bytes 3170312 | tf_op jit(solution)/shard_map/ppermute | solution.py:693
  61.7 58.3 %copy-start.7 = (bf16[129,32,128]{2,1,0:T(8,128)(2,1)}, bf16[129,32,128]{2,1,0:T(8,128)(2,1)S(1)}, u32[]{:S(2)}) copy-start(bf16[129,32,128]{2,1,0:T(8,128)(2,1)S(1)} %collective-permute-done.1.push_ref) | copy-start | bytes 3170308
  61.7 58.3 %all-to-all-start.1 = ((bf16[128,2,32,128]{3,2,1,0:T(8,128)(2,1)}), bf16[128,2,32,128]{3,2,1,0:T(8,128)(2,1)S(1)}, u32[]{:S(2)}, u32[]{:S(2)}) async-start(bf16[128,2,32,128]{3,2,1,0:T(8,128)(2,1)} %bitcast.26), calls=%async_computation.1 | async-start | bytes 4194304 | tf_op jit(solution)/shard_map/all_to_all | solution.py:699
  120.0 6.3 %copy-start.2 = (bf16[128,2,32,128]{3,2,1,0:T(8,128)(2,1)}, bf16[128,2,32,128]{3,2,1,0:T(8,128)(2,1)S(1)}, u32[]{:S(2)}) copy-start(bf16[128,2,32,128]{3,2,1,0:T(8,128)(2,1)S(1)} %all-to-all-done.1) | copy-start | bytes 6291460
  126.3 64.1 %collective-permute-start.2 = (bf16[128,128,256]{2,1,0:T(8,128)(2,1)}, bf16[128,128,256]{2,1,0:T(8,128)(2,1)}, u32[]{:S(2)}, u32[]{:S(2)}) collective-permute-start(bf16[128,128,256]{2,1,0:T(8,128)(2,1)} %recompute.3), channel_id=1, source_target_pairs={{0,4},{4,0},{8,12},{12,8},{16,20},{20,16},{24,28},{28,24},{32,36},... | collective-permute-start | bytes 25165832 | tf_op jit(solution)/shard_map/ppermute | solution.py:693
  147.4 42.9 %all-to-all-start.2 = ((f32[128,2,2,128]{3,2,1,0:T(2,128)}), f32[128,2,2,128]{3,2,1,0:T(2,128)S(1)}, u32[]{:S(2)}, u32[]{:S(2)}) async-start(f32[128,2,2,128]{3,2,1,0:T(2,128)} %bitcast.31), calls=%async_computation.2 | async-start | bytes 524288 | tf_op jit(solution)/shard_map/all_to_all | solution.py:699
  184.9 5.4 %collective-permute-start.3 = (f32[32,256]{1,0:T(8,128)}, f32[32,256]{1,0:T(8,128)S(1)}, u32[]{:S(2)}, u32[]{:S(2)}) collective-permute-start(f32[32,256]{1,0:T(8,128)} %get-tuple-element.66), channel_id=1, source_target_pairs={{4,0},{8,4},{12,8},{16,12},{20,16},{24,20},{28,24},{32,28},{36,32}... | collective-permute-start | bytes 98312 | tf_op jit(solution)/shard_map/ppermute | solution.py:689
  190.3 0.6 copy-start.5
  190.3 0.7 copy-start.3
